TPU v7x, 128 devices: a whole 4x4x4 slice. The times are simulated.
128 devices in a mesh: outer: 8 (over y, core), inner: 16 (over z, x).
Axes of the slice: x: 4, y: 4, z: 4, core: 2. Of those that a mesh axis runs over, the one named last changes fastest.
Arguments:
- entities: float32 [262144, 400], P(('outer', 'inner')), may hold values from -0.3 to 0.3
- panel_rows: float32 [16384, 400], P(('outer', 'inner')), may hold values from -0.3 to 0.3
- relations: float32 [240, 400], replicated, may hold values from -2 to 2
- source_owner: int32 [131072], P(('outer', 'inner')), may hold values from 0 to 127, as said below
- source_row: int32 [131072], P(('outer', 'inner')), may hold values from 0 to 2047
- relation_ids: int32 [131072], P(('outer', 'inner')), may hold values from 0 to 239
- target_ids: int32 [131072], P(('outer', 'inner')), may hold values from 0 to 2047
- negatives: int32 [128, 1024], P(('outer', 'inner')), may hold values from 0 to 2047
Outputs:
- entity_grad: float32 [262144, 400], P(('outer', 'inner'))
- panel_grad: float32 [16384, 400], P(('outer', 'inner'))
- relation_grad: float32 [240, 400], replicated
Inputs may be any that keep to these rules, and one draw needn't show every extreme that they name: `source_owner`: each device's edges name every device as owner at most 12 times; one device, the same for all, is named exactly 12 times by every device's edges.
All inputs are finite; a program needn't handle non-finite values.
Results may differ from a plain program's by a relative error of at most 0.0003.
Values sent between devices are 32-bit elements; how exact they have to be, the bound alone decides.
A program may use at most 128 MiB of HBM per device.

v0:
```python
import jax
import jax.numpy as jnp
from jax import lax
from jax.sharding import PartitionSpec as P


def block_grads(source_vecs, rel_scale, target_vecs, negative_vecs):
    query_vecs = source_vecs * rel_scale
    positive = jnp.sum(query_vecs * target_vecs, axis=1)
    scores = jnp.dot(
        query_vecs,
        negative_vecs.T,
        precision=lax.Precision.HIGHEST,
        preferred_element_type=jnp.float32,
    )
    pos_exp = jnp.exp(positive)
    neg_exp = jnp.exp(scores)
    denominator = pos_exp + jnp.sum(neg_exp, axis=1)
    pos_weight = pos_exp / denominator - 1.0
    neg_weight = neg_exp / denominator[:, None]
    grad_query = pos_weight[:, None] * target_vecs + jnp.dot(
        neg_weight,
        negative_vecs,
        precision=lax.Precision.HIGHEST,
        preferred_element_type=jnp.float32,
    )
    grad_negative = jnp.dot(
        neg_weight.T,
        query_vecs,
        precision=lax.Precision.HIGHEST,
        preferred_element_type=jnp.float32,
    )
    grad_target = pos_weight[:, None] * query_vecs
    return (grad_query, grad_negative, grad_target)


def on_device(
    entities, panel_rows, relations, source_owner, source_row, relation_ids, target_ids, negatives
):
    devices = lax.axis_size(("outer", "inner"))
    edge_count = source_owner.shape[0]
    features = entities.shape[1]
    capacity = max(2, 3 * edge_count // (2 * devices))
    blocks_here, neg_count = negatives.shape
    block_rows = edge_count // blocks_here
    owner_marks = (source_owner[:, None] == jnp.arange(devices, dtype=jnp.int32)[None, :]).astype(
        jnp.int32
    )
    slot_rank = jnp.sum((jnp.cumsum(owner_marks, axis=0) - 1) * owner_marks, axis=1)
    slot_ids = source_owner * capacity + slot_rank
    wanted = (
        jnp.zeros((devices * capacity,), jnp.int32)
        .at[slot_ids]
        .set(source_row)
        .reshape(devices, capacity)
    )
    requested = lax.all_to_all(wanted, ("outer", "inner"), split_axis=0, concat_axis=0, tiled=True)
    served = entities[requested]
    fetched = lax.all_to_all(served, ("outer", "inner"), split_axis=0, concat_axis=0, tiled=True)
    source_vecs = fetched.reshape(devices * capacity, features)[slot_ids]
    panel_all = lax.all_gather(panel_rows, "inner", axis=0, tiled=True)
    rel_scale = relations[relation_ids]
    target_vecs = panel_all[target_ids]
    negative_vecs = panel_all[negatives]
    grad_query, grad_negative, grad_target = lax.map(
        lambda pieces: block_grads(*pieces),
        (
            source_vecs.reshape(blocks_here, block_rows, features),
            rel_scale.reshape(blocks_here, block_rows, features),
            target_vecs.reshape(blocks_here, block_rows, features),
            negative_vecs,
        ),
    )
    grad_query = grad_query.reshape(edge_count, features)
    slot_grads = (
        jnp.zeros((devices * capacity, features), jnp.float32)
        .at[slot_ids]
        .add(grad_query * rel_scale)
    )
    slot_grads = slot_grads.reshape(devices, capacity, features)
    returned = lax.all_to_all(
        slot_grads, ("outer", "inner"), split_axis=0, concat_axis=0, tiled=True
    )
    entity_grad = (
        jnp.zeros_like(entities)
        .at[requested.reshape(-1)]
        .add(returned.reshape(devices * capacity, features))
    )
    panel_terms = (
        jnp.zeros_like(panel_all).at[target_ids].add(grad_target.reshape(edge_count, features))
    )
    panel_terms = panel_terms.at[negatives.reshape(-1)].add(
        grad_negative.reshape(blocks_here * neg_count, features)
    )
    panel_grad = lax.psum_scatter(panel_terms, "inner", scatter_dimension=0, tiled=True)
    rel_marks = (
        relation_ids[:, None] == jnp.arange(relations.shape[0], dtype=jnp.int32)[None, :]
    ).astype(jnp.float32)
    rel_terms = jnp.dot(
        rel_marks.T,
        grad_query * source_vecs,
        precision=lax.Precision.HIGHEST,
        preferred_element_type=jnp.float32,
    )
    relation_grad = lax.psum(rel_terms, ("outer", "inner"))
    return (entity_grad, panel_grad, relation_grad)


def solution(mesh):
    placed = (
        P(("outer", "inner"), None),
        P(("outer", "inner"), None),
        P(),
        P(("outer", "inner")),
        P(("outer", "inner")),
        P(("outer", "inner")),
        P(("outer", "inner")),
        P(("outer", "inner"), None),
    )
    return jax.shard_map(
        on_device,
        mesh=mesh,
        in_specs=placed,
        out_specs=(P(("outer", "inner"), None), P(("outer", "inner"), None), P()),
        check_vma=False,
    )
```

profile of v0, /device:TPU:1, one launch (start us, length us, event | category | flops | bytes accessed | tf_op | source)
XLA Modules:
  0.0 462.7 jit_solution(5941525985860618500)
XLA Ops:
  7.2 1.9 copy.43
  9.2 0.8 copy.36
  10.0 0.2 fusion.11
  10.2 0.8 copy-done.2
  11.0 1.1 add_add_fusion
  12.2 0.4 fusion.9
  12.6 4.5 scatter_custom_fusion
  17.1 0.7 all_to_all.14
  17.8 11.5 %all-to-all-start = ((s32[128,1,12]{2,1,0:T(1,128)}), s32[128,1,12]{2,1,0:T(1,128)S(1)}, u32[]{:S(2)}, u32[]{:S(2)}) async-start(s32[128,1,12]{2,1,0:T(1,128)} %bitcast.4), calls=%async_computation | async-start | bytes 131072 | tf_op jit(solution)/shard_map/all_to_all | solution.py:57
  29.3 3.3 copy.39
  32.7 6.4 %all-to-all-done = s32[128,1,12]{2,1,0:T(1,128)S(1)} async-done(((s32[128,1,12]{2,1,0:T(1,128)}), s32[128,1,12]{2,1,0:T(1,128)S(1)}, u32[]{:S(2)}, u32[]{:S(2)}) %all-to-all-start) | async-done | bytes 6176 | tf_op jit(solution)/shard_map/all_to_all | solution.py:57
  39.1 7.2 %gather_fusion = f32[1536,400]{1,0:T(8,128)S(1)} fusion(f32[2048,400]{1,0:T(8,128)} %copy.39, s32[2048]{0:T(1024)S(1)} %pad_clamp_fusion), kind=kCustom, calls=%fused_computation | custom fusion | bytes 4921344 | tf_op jit(solution)/shard_map/gather | solution.py:58
  46.3 2.2 reshape.169
  48.6 5.4 %all-to-all-start.1 = ((f32[128,12,400]{2,1,0:T(8,128)}), f32[128,12,400]{2,1,0:T(8,128)}, u32[]{:S(2)}, u32[]{:S(2)}) async-start(f32[128,12,400]{2,1,0:T(8,128)} %reshape.169), calls=%async_computation.1 | async-start | bytes 8388608 | tf_op jit(solution)/shard_map/all_to_all | solution.py:59
  54.0 0.2 reduce-scatter.2.cloned.1.call-start
  54.5 3.5 gather_fusion.2
  58.0 1.7 copy.42
  59.8 54.7 %all-to-all-done.1 = f32[128,12,400]{2,1,0:T(8,128)} async-done(((f32[128,12,400]{2,1,0:T(8,128)}), f32[128,12,400]{2,1,0:T(8,128)}, u32[]{:S(2)}, u32[]{:S(2)}) %all-to-all-start.1) | async-done | bytes 2457632 | tf_op jit(solution)/shard_map/all_to_all | solution.py:59
  114.4 3.0 reshape.164
  117.4 4.9 %gather_fusion.1 = f32[1024,400]{1,0:T(8,128)} fusion(f32[1536,400]{1,0:T(8,128)S(1)} %reshape.164, s32[1024]{0:T(1024)S(1)} %get-tuple-element.35), kind=kCustom, calls=%fused_computation.1 | custom fusion | bytes 3280896 | tf_op jit(solution)/shard_map/gather | solution.py:60
  122.3 1.8 copy.41
  124.1 7.5 %gather_fusion.3 = f32[1024,400]{1,0:T(8,128)} fusion(f32[2048,400]{1,0:T(8,128)} %all-gather.2.cloned.1.call-done, s32[1024]{0:T(1024)S(1)} %get-tuple-element.40), kind=kCustom, calls=%fused_computation.3 | custom fusion | bytes 3280896 | tf_op jit(solution)/shard_map/gather | solution.py:63
  131.6 2.8 copy.44
  134.4 2.4 multiply_reduce_fusion
  136.8 7.5 %gather_fusion.4 = f32[1024,400]{1,0:T(8,128)} fusion(f32[2048,400]{1,0:T(8,128)} %all-gather.2.cloned.1.call-done, s32[1024]{0:T(1024)S(1)} %broadcast_clamp_fusion), kind=kCustom, calls=%fused_computation.4 | custom fusion | bytes 3280896 | tf_op jit(solution)/shard_map/gather | solution.py:64
  144.2 9.5 %exponential_reduce_fusion = (f32[1024]{0:T(1024)S(1)}, f32[1024,1024]{0,1:T(8,128)}) fusion(f32[1024,400]{0,1:T(8,128)S(1)} %get-tuple-element.34, f32[1024,400]{1,0:T(8,128)} %gather_fusion.4), kind=kOutput, calls=%fused_computation.11 | convolution fusion | flops 5034212352 | bytes 7475200 | tf_op jit(solution)/shard_map/while/body/eval_jaxpr/dot_general | solution.py:10
  153.8 1.4 broadcast_multiply_fusion
  155.1 2.8 copy.48
  158.0 9.8 %fusion.8 = f32[1024,400]{1,0:T(8,128)} fusion(f32[1024,400]{0,1:T(8,128)S(1)} %get-tuple-element.34, f32[1024,1024]{0,1:T(8,128)} %get-tuple-element.42, f32[1024]{0:T(1024)S(1)} %get-tuple-element.38), kind=kOutput, calls=%fused_computation.22 | convolution fusion | flops 5034213376 | bytes 7475200 | tf_op jit(solution)/shard_map/while/body/eval_jaxpr/dot_general | solution.py:27
  167.8 9.7 %scatter_custom_fusion.3 = f32[2048,400]{1,0:T(8,128)} fusion(s32[1024]{0:T(1024)S(1)} %get-tuple-element.39, f32[1024,400]{1,0:T(8,128)} %copy.48, f32[]{:T(128)} %constant.16.clone.1), kind=kCustom, calls=%fused_computation.12 | custom fusion | flops 409600 | bytes 3277312 | tf_op jit(solution)/shard_map/scatter-add | solution.py:90
  177.4 11.4 %scatter_fusion = f32[2048,400]{1,0:T(8,128)} fusion(f32[2048,400]{1,0:T(8,128)} %scatter_custom_fusion.3, s32[1024]{0:T(1024)S(1)} %bitcast.24, f32[1024,400]{1,0:T(8,128)} %fusion.8), kind=kCustom, calls=%fused_computation.9 | custom fusion | flops 409600 | bytes 4919296 | tf_op jit(solution)/shard_map/scatter-add | solution.py:92
  188.8 1.4 copy-done
  190.2 12.1 %fusion.18 = (f32[1024,400]{0,1:T(8,128)}, f32[1024,400]{0,1:T(8,128)}) fusion(f32[1024,400]{0,1:T(8,128)S(1)} %copy-done, f32[1024,400]{1,0:T(8,128)} %gather_fusion.4, f32[1024,1024]{0,1:T(8,128)} %get-tuple-element.42, f32[1024]{0:T(1024)S(1)} %get-tuple-element.38, f32[1024,400]{0,1:T(8,128)} %copy.44, f32[1024]{0:T(1024)S(1)} %get-tuple-element.37), kind=kOutput, calls=%fused_computation.52 | convolution fusion | flops 5035442176 | bytes 12394496 | tf_op jit(solution)/shard_map/while/body/eval_jaxpr/dot_general | solution.py:21
  202.3 2.9 copy.47
  205.2 9.1 %scatter_custom_fusion.1 = f32[1536,400]{1,0:T(8,128)} fusion(s32[1024]{0:T(1024)S(1)} %get-tuple-element.36, f32[1024,400]{1,0:T(8,128)} %copy.47, f32[]{:T(128)} %constant.16.clone.1), kind=kCustom, calls=%fused_computation.20 | custom fusion | flops 409600 | bytes 2458112 | tf_op jit(solution)/shard_map/scatter-add | solution.py:78
  214.3 4.7 %reshape.165 = f32[128,12,400]{2,1,0:T(8,128)} reshape(f32[1536,400]{1,0:T(8,128)} %scatter_custom_fusion.1) | data formatting | bytes 4915200 | tf_op jit(solution)/shard_map/reshape | solution.py:80
  219.0 5.2 %all-to-all-start.2 = ((f32[128,12,400]{2,1,0:T(8,128)}), f32[128,12,400]{2,1,0:T(8,128)}, u32[]{:S(2)}, u32[]{:S(2)}) async-start(f32[128,12,400]{2,1,0:T(8,128)} %reshape.165), calls=%async_computation.2 | async-start | bytes 8388608 | tf_op jit(solution)/shard_map/all_to_all | solution.py:81
  224.2 1.9 fusion.4
  226.1 0.5 broadcast.156
  226.6 0.8 reduce.5
  227.6 51.0 %all-to-all-done.2 = f32[128,12,400]{2,1,0:T(8,128)} async-done(((f32[128,12,400]{2,1,0:T(8,128)}), f32[128,12,400]{2,1,0:T(8,128)}, u32[]{:S(2)}, u32[]{:S(2)}) %all-to-all-start.2) | async-done | bytes 2457632 | tf_op jit(solution)/shard_map/all_to_all | solution.py:81
  278.6 3.0 reshape.228
  281.6 11.8 %scatter_custom_fusion.2 = f32[2048,400]{1,0:T(8,128)} fusion(s32[1536]{0:T(1024)S(1)} %fusion.14, f32[1536,400]{1,0:T(8,128)S(1)} %reshape.228, f32[]{:T(128)} %constant.16.clone.1), kind=kCustom, calls=%fused_computation.14 | custom fusion | flops 614400 | bytes 3276804 | tf_op jit(solution)/shard_map/scatter-add | solution.py:87
  293.4 5.2 %copy.51 = f32[2048,400]{0,1:T(8,128)} copy(f32[2048,400]{1,0:T(8,128)} %scatter_custom_fusion.2) | data formatting | bytes 6553600
  298.6 5.9 %reduce-scatter.2.cloned.1.call-done = f32[128,400]{1,0:T(8,128)} async-done(((f32[2048,400]{1,0:T(8,128)}), f32[128,400]{1,0:T(8,128)}) %reduce-scatter.2.cloned.1.call-update) | async-done | bytes 204816 | tf_op jit(solution)/shard_map/reduce_scatter | solution.py:95
  304.5 1.8 copy.52
  306.3 148.0 %all-reduce.2.cloned.1.call-done = f32[240,400]{0,1:T(8,128)} async-done(((f32[240,400]{0,1:T(8,128)}), f32[240,400]{0,1:T(8,128)}) %all-reduce.2.cloned.1.call-update) | async-done | bytes 384016 | tf_op jit(solution)/shard_map/psum | solution.py:105
  454.3 1.8 copy.56
  (39 shorter events, 0.8 us)
Async XLA Ops:
  7.2 5.0 %copy-start.5 = (s32[1024]{0:T(1024)S(1)}, s32[1024]{0:T(1024)}, u32[]{:S(2)}) copy-start(s32[1024]{0:T(1024)} %param.11) | copy-start | bytes 12292
  7.2 22.1 %copy-start.1 = (f32[2048,400]{0,1:T(8,128)S(1)}, f32[2048,400]{0,1:T(8,128)}, u32[]{:S(2)}) copy-start(f32[2048,400]{0,1:T(8,128)} %param.8) | copy-start | bytes 9830404
  7.2 116.9 %all-gather.2.cloned.1.call-start = ((), (), s32[]{:S(2)}) async-start(), calls=%async_computation.4 | async-start | bytes 4456448 | tf_op jit(solution)/shard_map/all_gather | solution.py:61
  10.2 0.8 copy-start.2
  17.8 21.2 %all-to-all-start = ((s32[128,1,12]{2,1,0:T(1,128)}), s32[128,1,12]{2,1,0:T(1,128)S(1)}, u32[]{:S(2)}, u32[]{:S(2)}) async-start(s32[128,1,12]{2,1,0:T(1,128)} %bitcast.4), calls=%async_computation | async-start | bytes 131072 | tf_op jit(solution)/shard_map/all_to_all | solution.py:57
  48.5 5.7 %copy-start.4 = (f32[240,400]{0,1:T(8,128)S(1)}, f32[240,400]{0,1:T(8,128)}, u32[]{:S(2)}) copy-start(f32[240,400]{0,1:T(8,128)} %param.10) | copy-start | bytes 1152004
  48.5 5.9 %copy-start.7 = (s32[1024]{0:T(1024)S(1)}, s32[1024]{0:T(1024)}, u32[]{:S(2)}) copy-start(s32[1024]{0:T(1024)} %param.13) | copy-start | bytes 12292
  48.6 65.9 %all-to-all-start.1 = ((f32[128,12,400]{2,1,0:T(8,128)}), f32[128,12,400]{2,1,0:T(8,128)}, u32[]{:S(2)}, u32[]{:S(2)}) async-start(f32[128,12,400]{2,1,0:T(8,128)} %reshape.169), calls=%async_computation.1 | async-start | bytes 8388608 | tf_op jit(solution)/shard_map/all_to_all | solution.py:59
  54.0 250.5 %reduce-scatter.2.cloned.1.call-start = ((), (), s32[]{:S(2)}) async-start(), calls=%async_computation.5 | async-start | bytes 4456448 | tf_op jit(solution)/shard_map/reduce_scatter | solution.py:95
  58.0 1.7 copy-start.6
  58.0 1.8 copy-start.8
  188.8 1.4 copy-start
  219.0 5.3 %copy-start.3 = (f32[1024,400]{0,1:T(8,128)S(1)}, f32[1024,400]{0,1:T(8,128)}, u32[]{:S(2)}) copy-start(f32[1024,400]{0,1:T(8,128)} %get-tuple-element.44) | copy-start | bytes 4915204
  219.0 59.7 %all-to-all-start.2 = ((f32[128,12,400]{2,1,0:T(8,128)}), f32[128,12,400]{2,1,0:T(8,128)}, u32[]{:S(2)}, u32[]{:S(2)}) async-start(f32[128,12,400]{2,1,0:T(8,128)} %reshape.165), calls=%async_computation.2 | async-start | bytes 8388608 | tf_op jit(solution)/shard_map/all_to_all | solution.py:81
  224.2 230.2 %all-reduce.2.cloned.1.call-start = ((), (), s32[]{:S(2)}) async-start(), calls=%async_computation.6 | async-start | bytes 819200 | tf_op jit(solution)/shard_map/psum | solution.py:105
Sparse Core Ops, SparseCore 0:
  10.7 89.1 all-gather.1
  188.9 115.5 reduce-scatter.1
  310.6 143.6 all-reduce.1
where the time goes:
time: 464 us; the launch traced here: 463 us
  waiting for transfers between devices  266 us (57%)
  local copies, waits for them, and re-layouts  78.6 us (17%)
  other arithmetic  48.3 us (10%)
  matrix products  33.2 us (7%)
  starting transfers between devices  22.4 us (5%)
  between operations  14 us (3%)
    psum x1, waiting for transfers between devices, on_device(): relation_grad = lax.psum(rel_terms, ('outer', 'inner'))  148 us
    all_to_all x1, waiting for transfers between devices, on_device(): lax.all_to_all(served, ('outer', 'inner'), split_axis=0, concat_axis=0, t...  54.7 us
    all_to_all x1, waiting for transfers between devices, on_device(): lax.all_to_all(slot_grads, ('outer', 'inner'), split_axis=0, concat_axis=...  51 us
    unnamed x24, local copies, waits for them, and re-layouts  16.4 us
    dot_general x1, matrix products, block_grads(): jnp.dot(neg_weight, negative_vecs, precision=lax.Precision.HIGHEST, prefe...  12.1 us
    scatter-add x1, other arithmetic, on_device(): entity_grad = jnp.zeros_like(entities).at[requested.reshape(-1)].add(retu...  11.8 us
    all_to_all x1, starting transfers between devices, on_device(): lax.all_to_all(wanted, ('outer', 'inner'), split_axis=0, concat_axis=0, t...  11.5 us
    scatter-add x1, other arithmetic, on_device(): panel_terms.at[negatives.reshape(-1)]  11.4 us
  transfers between devices with their start and end apart: 6, of which 5 were waited for; matrix products, arithmetic and copies ran while one was open for 19% of the time, Pallas kernels for 0%

commit v1 on v0

v1 whole, which is shorter than its diff:
```python
import jax
import jax.numpy as jnp
from jax import lax
from jax.experimental import pallas as pl
from jax.experimental.pallas import tpu as pltpu
from jax.sharding import PartitionSpec as P

MESH = pl.DeviceIdType.MESH
F32, BF16, I32 = jnp.float32, jnp.bfloat16, jnp.int32

D, DP = 400, 512
HALF = 200
RELS = 240
ROWS = 2048
PANEL = 128
EDGES = 1024
CAP = 12
NO, NI = 8, 16
DEV = NO * NI
SLOTS = CAP * DEV
MSG = 40
BM = 256

NN = (((1,), (0,)), ((), ()))
NT = (((1,), (1,)), ((), ()))


def dot(a, b, dims=NN):
    return lax.dot_general(a, b, dims, preferred_element_type=F32)


def split(x):
    hi = x.astype(BF16)
    return hi, (x - hi.astype(F32)).astype(BF16)


def iota(shape, dim):
    return lax.broadcasted_iota(I32, shape, dim)


def mark(cond):
    return jnp.where(cond, 1.0, 0.0).astype(BF16)


def step_kernel(
    ent_ref, pan_ref, rel_ref, owner_ref, srow_ref, rid_ref, tid_ref, neg_ref,
    eout_ref, pout_ref, rout_ref,
    entf, eh, el, want, tgt_t, rel_t, r1, s2, r2,
    pan_all, ph, plo, relh, rell, cnt,
    send_buf, fetched, returned, xs, gs, onehot, tcol, rcol,
    scores, wh, wl, acc, relacc,
    rsa1, rsb1, sa, sb, rsa2, rsb2,
    ra1, a1p, ra2, a3s, a3, c4,
    local_sem, all_in,
    i1s, i1r, i2s, i2r, g1s, g1r, g2s, g2r, fs, fr, bs, br,
    p1s, p1r, p2s, p2r, q1s, q1r, q2s, q2r, q3s, q3r, q4s, q4r,
):
    o, i = lax.axis_index("outer"), lax.axis_index("inner")
    me = o * NI + i
    mine = i * NO + o
    z, x = i >> 2, i & 3
    y, c = o >> 1, o & 1

    def outer_peer(d):
        return (o + d) & 7

    def inner_peer(d):
        return (i + d) & 15

    def xp(d):
        return (z << 2) + ((x + d) & 3)

    def zp(d):
        return (((z + d) & 3) << 2) + x

    def remote(src, dst, ss, rs, po, pi):
        return pltpu.make_async_remote_copy(
            src_ref=src, dst_ref=dst, send_sem=ss, recv_sem=rs,
            device_id=(po, pi), device_id_type=MESH,
        )

    barrier = pltpu.get_barrier_semaphore()

    def greet_outer(d, carry):
        pl.semaphore_signal(barrier, inc=1, device_id=(outer_peer(d), i), device_id_type=MESH)
        return carry

    def greet_inner(d, carry):
        pl.semaphore_signal(barrier, inc=1, device_id=(o, inner_peer(d)), device_id_type=MESH)
        return carry

    lax.fori_loop(1, NO, greet_outer, 0)
    lax.fori_loop(1, NI, greet_inner, 0)
    load = pltpu.make_async_copy(ent_ref, entf, local_sem.at[0])
    load.start()

    owner = owner_ref[...]
    owned = owner == iota((DEV, EDGES), 0)
    owned_b = mark(owned)
    before = mark(iota((EDGES, EDGES), 0) < iota((EDGES, EDGES), 1))
    rank = jnp.sum(jnp.where(owned, dot(owned_b, before), 0.0), axis=0, keepdims=True)
    at_rank = rank.astype(I32) == iota((16, EDGES), 0)

    def table(values):
        return dot(owned_b, jnp.where(at_rank, values.astype(F32), 0.0).astype(BF16), NT)

    named = (table(jnp.ones((1, EDGES), I32)) - 1.0) * 8192.0
    srow, tid = srow_ref[...], tid_ref[...]
    want[...] = jnp.zeros_like(want)
    want[:, 0:16] = table(srow >> 4) * 16.0 + table(srow & 15) + named
    tgt_t[...] = table(tid >> 4) * 16.0 + table(tid & 15) + named
    rel_t[...] = table(rid_ref[...]) + named

    pl.semaphore_wait(barrier, NO - 1 + NI - 1)

    def send_i1(d, carry):
        po = outer_peer(d)
        remote(
            want.at[pl.ds(pl.multiple_of(po * NI, 8), NI)],
            r1.at[pl.ds(pl.multiple_of(o * NI, 8), NI)],
            i1s, i1r, po, i,
        ).start()
        return carry

    lax.fori_loop(1, NO, send_i1, 0)
    r1[pl.ds(pl.multiple_of(o * NI, 8), NI), :] = want[pl.ds(pl.multiple_of(o * NI, 8), NI), :]

    halves = (pl.ds(0, HALF), pl.ds(HALF, HALF))
    first = []
    for d in (1, 3, 2):
        for h, peer in enumerate((xp, zp)):
            cp = remote(
                pan_ref.at[halves[h]], pan_all.at[i, halves[h]],
                g1s.at[h, d - 1], g1r.at[h, d - 1], o, peer(d),
            )
            cp.start()
            first.append(cp)
    own_pan = pltpu.make_async_copy(pan_ref, pan_all.at[i], local_sem.at[1])
    own_pan.start()

    n1 = (NO - 1) * NI
    w1 = remote(want.at[pl.ds(0, n1)], r1.at[pl.ds(0, n1)], i1s, i1r, outer_peer(1), i)
    w1.wait_recv()
    for k in range(NI):
        s2[k * NO:(k + 1) * NO, :] = r1[pl.ds(k, NO, stride=NI), :]

    def send_i2(d, carry):
        pi = inner_peer(d)
        remote(
            s2.at[pl.ds(pl.multiple_of(pi * NO, 8), NO)],
            r2.at[pl.ds(pl.multiple_of(i * NO, 8), NO)],
            i2s, i2r, o, pi,
        ).start()
        return carry

    lax.fori_loop(1, NI, send_i2, 0)
    r2[pl.ds(pl.multiple_of(i * NO, 8), NO), :] = s2[pl.ds(pl.multiple_of(i * NO, 8), NO), :]
    second = []
    for d in (1, 3, 2):
        for h, peer in enumerate((zp, xp)):
            cp = remote(
                pan_ref.at[halves[h]], pan_all.at[i, halves[h]],
                g2s.at[h, 0, d - 1], g2r.at[h, 0, d - 1], o, peer(d),
            )
            cp.start()
            second.append(cp)

    load.wait()
    eh[D:DP, :] = jnp.zeros((DP - D, ROWS), BF16)
    el[D:DP, :] = jnp.zeros((DP - D, ROWS), BF16)

    def split_ent(j, carry):
        rows = pl.ds(pl.multiple_of(j * 16, 16), 16)
        hi, lo = split(entf[rows, :])
        eh[rows, :] = hi
        el[rows, :] = lo
        return carry

    lax.fori_loop(0, D // 16, split_ent, 0)

    n2 = (NI - 1) * NO
    w2 = remote(s2.at[pl.ds(0, n2)], r2.at[pl.ds(0, n2)], i2s, i2r, o, inner_peer(1))
    w2.wait_recv()

    for e in (1, 3, 2):
        for h in (0, 1):
            near, far = ((xp, zp), (zp, xp))[h]
            src = near(-e)
            remote(
                pan_ref.at[halves[h]], pan_all.at[src, halves[h]],
                g1s.at[h, e - 1], g1r.at[h, e - 1], o, src,
            ).wait_recv()
            for d in (1, 3, 2):
                cp = remote(
                    pan_all.at[src, halves[h]], pan_all.at[src, halves[h]],
                    g2s.at[h, e, d - 1], g2r.at[h, e, d - 1], o, far(d),
                )
                cp.start()
                second.append(cp)

    for j in range(3):
        for kk in range(4):
            k = 4 * j + kk
            ids = r2[:, k:k + 1].astype(I32)
            onehot[k * DEV:(k + 1) * DEV, :] = mark(ids == iota((DEV, ROWS), 1))
        rows = pl.ds(j * 4 * DEV, 4 * DEV)
        xs[rows, :] = dot(onehot[rows, :], eh[...], NT) + dot(onehot[rows, :], el[...], NT)

    def pack(src, dst):
        for k in range(CAP):
            for t in range(3):
                dst[pl.ds(3 * k + t, DEV, stride=MSG), :] = src[
                    k * DEV:(k + 1) * DEV, t * 128:(t + 1) * 128
                ]
        for half, ks in ((36, range(0, 8)), (37, range(8, CAP))):
            rest = None
            for k in ks:
                part = src[k * DEV:(k + 1) * DEV, 384:512]
                if k % 8:
                    part = pltpu.roll(part, 16 * (k % 8), 1)
                rest = part if rest is None else rest + part
            dst[pl.ds(half, DEV, stride=MSG), :] = rest

    def unpack(src, dst):
        tail = iota((DEV, 128), 1) < 16
        for k in range(CAP):
            for t in range(3):
                dst[k * DEV:(k + 1) * DEV, t * 128:(t + 1) * 128] = src[
                    pl.ds(3 * k + t, DEV, stride=MSG), :
                ]
            part = src[pl.ds(36 + k // 8, DEV, stride=MSG), :]
            if k % 8:
                part = pltpu.roll(part, 128 - 16 * (k % 8), 1)
            dst[k * DEV:(k + 1) * DEV, 384:512] = jnp.where(tail, part, 0.0)

    send_buf[pl.ds(38, DEV, stride=MSG), :] = jnp.zeros((DEV, 128), F32)
    send_buf[pl.ds(39, DEV, stride=MSG), :] = jnp.zeros((DEV, 128), F32)
    pack(xs, send_buf)

    def other(j):
        t, dc, b, a = j & 3, (j >> 2) & 1, (j >> 3) & 3, (j >> 5) & 3
        po = (((y + t + a) & 3) << 1) + ((c + dc) & 1)
        pi = (((z + t + b) & 3) << 2) + ((x + t) & 3)
        return po, pi

    def message(buf, n):
        return buf.at[pl.ds(pl.multiple_of(n * MSG, 8), MSG)]

    def send_rows(j, carry):
        po, pi = other(j)
        remote(message(send_buf, pi * NO + po), message(fetched, me), fs, fr, po, pi).start()
        return carry

    lax.fori_loop(1, DEV, send_rows, 0)
    own_rows = pltpu.make_async_copy(
        message(send_buf, mine), message(fetched, me), local_sem.at[2]
    )
    own_rows.start()

    neg = neg_ref[...]
    cnt[...] = dot(
        mark((neg >> 7) == iota((NI, EDGES), 0)), mark((neg & 127) == iota((PANEL, EDGES), 0)), NT
    )
    relh[...] = jnp.zeros_like(relh)
    rell[...] = jnp.zeros_like(rell)
    hi, lo = split(rel_ref[...])
    relh[0:D, 0:RELS] = hi
    rell[0:D, 0:RELS] = lo
    for k in range(CAP):
        rows = pl.ds(k * DEV, DEV)
        tcol[rows, :] = jnp.broadcast_to(tgt_t[:, k:k + 1], (DEV, 128)).astype(I32)
        rcol[rows, :] = jnp.broadcast_to(rel_t[:, k:k + 1], (DEV, 128)).astype(I32)
    ph[D:DP, :] = jnp.zeros((DP - D, ROWS), BF16)
    plo[D:DP, :] = jnp.zeros((DP - D, ROWS), BF16)
    relacc[...] = jnp.zeros_like(relacc)
    acc[...] = jnp.zeros_like(acc)

    own_pan.wait()
    for cp in first:
        cp.wait_send()
    for cp in second:
        cp.wait()
    for b in range(NI):
        hi, lo = split(pan_all[b])
        ph[0:D, b * PANEL:(b + 1) * PANEL] = hi
        plo[0:D, b * PANEL:(b + 1) * PANEL] = lo

    own_rows.wait()
    n3 = (DEV - 1) * MSG
    w3 = remote(send_buf.at[pl.ds(0, n3)], fetched.at[pl.ds(0, n3)], fs, fr, outer_peer(1), i)
    w3.wait_recv()
    w3.wait_send()
    w1.wait_send()
    w2.wait_send()
    unpack(fetched, xs)

    def block(j, carry):
        base = pl.multiple_of(j * BM, BM)
        rows = pl.ds(base, BM)
        rel_mark = mark(rcol[rows, 0:1] == iota((BM, 256), 1))
        rel_rows = dot(rel_mark, relh[...], NT) + dot(rel_mark, rell[...], NT)
        query = xs[rows, :] * rel_rows
        qh, ql = split(query)
        scores[...] = dot(qh, ph[...]) + dot(qh, plo[...]) + dot(ql, ph[...])

        def weigh(n, inner_carry):
            part = pl.ds(pl.multiple_of(n * 16, 16), 16)
            ids = tcol[pl.ds(pl.multiple_of(base + n * 16, 16), 16), :]
            total = jnp.zeros((16, 128), F32)
            picked = jnp.zeros((16, 128), F32)
            terms, hits = [], []
            for b in range(NI):
                s = scores[part, b * PANEL:(b + 1) * PANEL]
                hit = ids == iota((16, PANEL), 1) + b * PANEL
                e = jnp.exp(s) * cnt[b:b + 1, :]
                total += e
                picked += jnp.where(hit, s, 0.0)
                terms.append(e)
                hits.append(hit)
            z0 = jnp.sum(total, axis=1, keepdims=True)
            inv = 1.0 / (z0 + jnp.exp(jnp.sum(picked, axis=1, keepdims=True)))
            for b in range(NI):
                w = (terms[b] - jnp.where(hits[b], z0, 0.0)) * inv
                w_hi, w_lo = split(w)
                wh[part, b * PANEL:(b + 1) * PANEL] = w_hi
                wl[part, b * PANEL:(b + 1) * PANEL] = w_lo
            return inner_carry

        lax.fori_loop(0, BM // 16, weigh, 0)
        grad = dot(wh[...], ph[...], NT) + dot(wh[...], plo[...], NT) + dot(wl[...], ph[...], NT)
        gs[rows, :] = grad * rel_rows
        gh, gl = split((grad * xs[rows, :]).T[0:D])
        relacc[0:D, :] += dot(gh, rel_mark) + dot(gl, rel_mark)
        th, tl = split(query.T[0:D])
        for b in range(0, NI, 2):
            lanes = slice(b * PANEL, (b + 2) * PANEL)
            add = dot(th, wh[:, lanes]) + dot(th, wl[:, lanes]) + dot(tl, wh[:, lanes])
            acc[b // 4, b % 4] += add[:, 0:PANEL]
            acc[b // 4, b % 4 + 1] += add[:, PANEL:2 * PANEL]
        return carry

    lax.fori_loop(0, SLOTS // BM, block, 0)

    reduce1 = []
    for d in (1, 3, 2):
        cp = remote(
            acc.at[(z + d) & 3, :, halves[0]], rsa1.at[d - 1],
            p1s.at[0, d - 1], p1r.at[0, d - 1], o, zp(d),
        )
        cp.start()
        reduce1.append(cp)
        cp = remote(
            acc.at[:, (x + d) & 3, halves[1]], rsb1.at[d - 1],
            p1s.at[1, d - 1], p1r.at[1, d - 1], o, xp(d),
        )
        cp.start()
        reduce1.append(cp)

    def send_q1(d, carry):
        po = outer_peer(d)
        remote(
            relacc.at[pl.ds(pl.multiple_of(po * 64, 8), 64)], ra1.at[o], q1s, q1r, po, i
        ).start()
        return carry

    lax.fori_loop(1, NO, send_q1, 0)
    ra1[o] = relacc[pl.ds(pl.multiple_of(o * 64, 8), 64), :]

    pack(gs, send_buf)

    def send_grads(j, carry):
        po, pi = other(j)
        remote(
            message(send_buf, po * NI + pi), message(returned, mine), bs, br, po, pi
        ).start()
        return carry

    lax.fori_loop(1, DEV, send_grads, 0)
    own_grads = pltpu.make_async_copy(
        message(send_buf, me), message(returned, mine), local_sem.at[3]
    )
    own_grads.start()

    v1 = remote(ra1.at[pl.ds(0, NO - 1)], ra1.at[pl.ds(0, NO - 1)], q1s, q1r, outer_peer(1), i)
    v1.wait_recv()
    part = ra1[0]
    for n in range(1, NO):
        part = part + ra1[n]
    for n in range(NI):
        a1p[n] = part[8 * (n >> 1):8 * (n >> 1) + 8, 128 * (n & 1):128 * (n & 1) + 128]

    def send_q2(d, carry):
        pi = inner_peer(d)
        remote(a1p.at[pi], ra2.at[i], q2s, q2r, o, pi).start()
        return carry

    lax.fori_loop(1, NI, send_q2, 0)
    ra2[i] = a1p[i]

    for cp in reduce1:
        cp.wait()
    sa[...] = acc[z, :, 0:HALF] + rsa1[0] + rsa1[1] + rsa1[2]
    sb[...] = acc[:, x, HALF:D] + rsb1[0] + rsb1[1] + rsb1[2]
    reduce2 = []
    for d in (1, 3, 2):
        cp = remote(
            sa.at[(x + d) & 3], rsa2.at[d - 1], p2s.at[0, d - 1], p2r.at[0, d - 1], o, xp(d)
        )
        cp.start()
        reduce2.append(cp)
        cp = remote(
            sb.at[(z + d) & 3], rsb2.at[d - 1], p2s.at[1, d - 1], p2r.at[1, d - 1], o, zp(d)
        )
        cp.start()
        reduce2.append(cp)

    v2 = remote(a1p.at[pl.ds(0, NI - 1)], ra2.at[pl.ds(0, NI - 1)], q2s, q2r, o, inner_peer(1))
    v2.wait_recv()
    part = ra2[0]
    for n in range(1, NI):
        part = part + ra2[n]
    a3s[...] = part
    a3[i] = part

    def send_q3(d, carry):
        pi = inner_peer(d)
        remote(a3s, a3.at[i], q3s, q3r, o, pi).start()
        return carry

    lax.fori_loop(1, NI, send_q3, 0)
    v3 = remote(a1p.at[pl.ds(0, NI - 1)], a3.at[pl.ds(0, NI - 1)], q3s, q3r, o, inner_peer(1))
    v3.wait_recv()
    for n in range(NI):
        c4[o, 8 * (n >> 1):8 * (n >> 1) + 8, 128 * (n & 1):128 * (n & 1) + 128] = a3[n]

    def send_q4(d, carry):
        po = outer_peer(d)
        remote(c4.at[o], c4.at[o], q4s, q4r, po, i).start()
        return carry

    lax.fori_loop(1, NO, send_q4, 0)

    own_grads.wait()
    w4 = remote(send_buf.at[pl.ds(0, n3)], returned.at[pl.ds(0, n3)], bs, br, outer_peer(1), i)
    w4.wait_recv()
    unpack(returned, xs)
    for j in range(3):
        rows = pl.ds(j * DP, DP)
        th, tl = split(xs[rows, :].T[0:D])
        for b in range(0, NI, 4):
            lanes = slice(b * PANEL, (b + 4) * PANEL)
            add = dot(th, onehot[rows, lanes]) + dot(tl, onehot[rows, lanes])
            if j == 0:
                entf[:, lanes] = add
            else:
                entf[:, lanes] += add
    store = pltpu.make_async_copy(entf, eout_ref, local_sem.at[4])
    store.start()

    for cp in reduce2:
        cp.wait()
    pout_ref[0:HALF, :] = sa[x] + rsa2[0] + rsa2[1] + rsa2[2]
    pout_ref[HALF:D, :] = sb[z] + rsb2[0] + rsb2[1] + rsb2[2]

    v4 = remote(c4.at[pl.ds(0, NO - 1)], c4.at[pl.ds(0, NO - 1)], q4s, q4r, outer_peer(1), i)
    v4.wait_recv()
    for n in range(NO - 1):
        top = min(D, (n + 1) * 64)
        rout_ref[n * 64:top, :] = c4[n, 0:top - n * 64, 0:RELS]

    w4.wait_send()
    v1.wait_send()
    v2.wait_send()
    v3.wait_send()
    v4.wait_send()
    store.wait()


def on_device(
    entities, panel_rows, relations, source_owner, source_row, relation_ids, target_ids, negatives
):
    dma, vm = pltpu.SemaphoreType.DMA, pltpu.VMEM
    scratch = [
        vm((D, ROWS), F32), vm((DP, ROWS), BF16), vm((DP, ROWS), BF16),
        vm((DEV, 128), F32), vm((DEV, 16), F32), vm((DEV, 16), F32),
        vm((DEV, 128), F32), vm((DEV, 128), F32), vm((DEV, 128), F32),
        vm((NI, D, PANEL), F32), vm((DP, ROWS), BF16), vm((DP, ROWS), BF16),
        vm((DP, 256), BF16), vm((DP, 256), BF16), vm((NI, PANEL), F32),
        vm((DEV * MSG, 128), F32), vm((DEV * MSG, 128), F32), vm((DEV * MSG, 128), F32),
        vm((SLOTS, DP), F32), vm((SLOTS, DP), F32), vm((SLOTS, ROWS), BF16),
        vm((SLOTS, 128), I32), vm((SLOTS, 128), I32),
        vm((BM, ROWS), F32), vm((BM, ROWS), BF16), vm((BM, ROWS), BF16),
        vm((4, 4, D, PANEL), F32), vm((DP, 256), F32),
        vm((3, 4, HALF, PANEL), F32), vm((3, 4, HALF, PANEL), F32),
        vm((4, HALF, PANEL), F32), vm((4, HALF, PANEL), F32),
        vm((3, HALF, PANEL), F32), vm((3, HALF, PANEL), F32),
        vm((NO, 64, 256), F32), vm((NI, 8, 128), F32), vm((NI, 8, 128), F32),
        vm((8, 128), F32), vm((NI, 8, 128), F32), vm((NO, 64, 256), F32),
        dma((5,)), pltpu.SemaphoreType.REGULAR,
        dma, dma, dma, dma,
        dma((2, 3)), dma((2, 3)), dma((2, 4, 3)), dma((2, 4, 3)),
        dma, dma, dma, dma,
        dma((2, 3)), dma((2, 3)), dma((2, 3)), dma((2, 3)),
        dma, dma, dma, dma, dma, dma, dma, dma,
    ]
    vmem = pl.BlockSpec(memory_space=pltpu.VMEM)
    anyw = pl.BlockSpec(memory_space=pl.ANY)
    entity, panel, relation = pl.pallas_call(
        step_kernel,
        out_shape=(
            jax.ShapeDtypeStruct((D, ROWS), F32),
            jax.ShapeDtypeStruct((D, PANEL), F32),
            jax.ShapeDtypeStruct((D, RELS), F32),
        ),
        in_specs=[anyw] + [vmem] * 7,
        out_specs=(anyw, vmem, vmem),
        scratch_shapes=scratch,
        compiler_params=pltpu.CompilerParams(
            collective_id=0, has_side_effects=True, vmem_limit_bytes=61 * 2**20
        ),
        name="edge_step",
    )(
        entities.T, panel_rows.T, relations.T,
        source_owner.reshape(1, EDGES), source_row.reshape(1, EDGES),
        relation_ids.reshape(1, EDGES), target_ids.reshape(1, EDGES), negatives,
    )
    return entity.T, panel.T, relation.T


def solution(mesh):
    placed = (
        P(("outer", "inner"), None),
        P(("outer", "inner"), None),
        P(),
        P(("outer", "inner")),
        P(("outer", "inner")),
        P(("outer", "inner")),
        P(("outer", "inner")),
        P(("outer", "inner"), None),
    )
    return jax.shard_map(
        on_device,
        mesh=mesh,
        in_specs=placed,
        out_specs=(P(("outer", "inner"), None), P(("outer", "inner"), None), P()),
        check_vma=False,
    )
```

time: 464 us -> 184 us (0.40)
  waiting for transfers between devices: 266 us -> 0 us
  Pallas kernels: 0 us -> 178 us
  local copies, waits for them, and re-layouts: 78.6 us -> 5.51 us
  other arithmetic: 48.3 us -> 0 us
  matrix products: 33.2 us -> 0 us
  starting transfers between devices: 22.4 us -> 0 us
  between operations: 14 us -> 0.66 us
    pallas_call x0 -> x1, Pallas kernels: none -> 178 us  [on_device(): pl.pallas_call(step_kernel, out_shape=(jax.ShapeDtypeStruct((D, ROWS), F3...]
    psum x1 -> x0, waiting for transfers between devices: 148 us -> none  [on_device(): relation_grad = lax.psum(rel_terms, ('outer', 'inner'))]
    all_to_all x3 -> x0, waiting for transfers between devices: 112 us -> none  [the longest x1 54.7 us: on_device(): lax.all_to_all(served, ('outer', 'inner'), split_axis=0, concat_axis=0, t...]
    scatter-add x4 -> x0, other arithmetic: 42 us -> none  [the longest x1 11.8 us: on_device(): entity_grad = jnp.zeros_like(entities).at[requested.reshape(-1)].add(retu...]
    gather x9 -> x0, local copies, waits for them, and re-layouts: 39 us -> none  [the longest x2 10.2 us: on_device(): target_vecs = panel_all[target_ids]]
    dot_general x4 -> x0, matrix products: 33.2 us -> none  [the longest x1 12.1 us: block_grads(): jnp.dot(neg_weight, negative_vecs, precision=lax.Precision.HIGHEST, prefe...]
    all_to_all x3 -> x0, starting transfers between devices: 22.1 us -> none  [the longest x1 11.5 us: on_device(): lax.all_to_all(wanted, ('outer', 'inner'), split_axis=0, concat_axis=0, t...]
    unnamed x24 -> x7, local copies, waits for them, and re-layouts: 16.4 us -> 5.51 us
  transfers between devices with their start and end apart: 6 -> 0, of which waited for: 5 -> 0; matrix products, arithmetic and copies ran while one was open for 19% -> 0% of each run, Pallas kernels for 0% -> 0%
where the time goes in v1:
time: 184 us
  Pallas kernels  178 us (97%)
  local copies, waits for them, and re-layouts  5.51 us (3%)
    pallas_call x1, Pallas kernels, on_device(): pl.pallas_call(step_kernel, out_shape=(jax.ShapeDtypeStruct((D, ROWS), F3...  178 us
    unnamed x7, local copies, waits for them, and re-layouts  5.51 us

profile of v1, /device:TPU:1, one launch (start us, length us, event | category | flops | bytes accessed | tf_op | source)
XLA Modules:
  0.0 184.3 jit_solution(9163833671555675876)
XLA Ops:
  0.6 178.1 %edge_step.1 = (f32[400,2048]{1,0:T(8,128)}, f32[400,128]{1,0:T(8,128)}, f32[400,240]{1,0:T(8,128)}) custom-call(f32[400,2048]{1,0:T(8,128)} %bitcast.11, f32[400,128]{1,0:T(8,128)} %bitcast.15, f32[400,240]{1,0:T(8,128)} %bitcast.12, s32[1,1024]{1,0:T(1,128)} %bitcast.16, s32[1,1024]{1,0:T(1,128)} %bitcast.17, s32[1,1024]{1,0:T(1,128)} %bitcast.18, ...), custom_call_target="tpu_custom_call" | custom-call | tf_op jit(solution)/shard_map/edge_step/pallas_call | solution.py:508
  178.7 0.0 copy-start.1
  178.8 0.0 copy-start
  178.8 4.1 %copy.14 = f32[2048,400]{0,1:T(8,128)} copy(f32[2048,400]{0,1:T(8,128)} %bitcast.10) | data formatting | bytes 6553600
  182.8 0.0 copy-done.1
  182.8 0.7 copy.15
  183.5 0.0 copy-done
  183.5 0.8 copy.16
Async XLA Ops:
  178.7 4.1 %copy-start.1 = (f32[400,128]{1,0:T(8,128)S(1)}, f32[400,128]{1,0:T(8,128)}, u32[]{:S(2)}) copy-start(f32[400,128]{1,0:T(8,128)} %get-tuple-element.7) | copy-start | bytes 614404
  178.8 4.8 %copy-start = (f32[400,240]{1,0:T(8,128)S(1)}, f32[400,240]{1,0:T(8,128)}, u32[]{:S(2)}) copy-start(f32[400,240]{1,0:T(8,128)} %get-tuple-element.8) | copy-start | bytes 1152004
